TPU v7x, 128 devices: a whole 4x4x4 slice. The times are simulated.
128 devices in a mesh: dev: 128 (over z, y, x, core).
Axes of the slice: x: 4, y: 4, z: 4, core: 2. Of those that a mesh axis runs over, the one named last changes fastest.
Arguments:
- blocks: bfloat16 [8192, 128, 128], P('dev'), may hold values from -6 to 6
- row_maps: bfloat16 [8192, 128, 128], P('dev'), may hold values from -0.5 to 0.5
- col_maps: bfloat16 [8192, 128, 128], P('dev'), may hold values from -0.5 to 0.5
- targets: int32 [8192, 1], P('dev'), may hold values from 0 to 127; in each aligned block of 64 rows (0 to 63, 64 to 127, ...) at most 2 rows name the same one
- date_index: int32 [8192], P('dev'), may hold values from 0 to 31
Outputs:
- coefficients: float32 [896, 128, 128], P('dev')
- residuals: bfloat16 [8192, 128, 128], P('dev')
Inputs may be any that keep to these rules, and one draw needn't show every extreme that they name: `targets`: among the 64 entries of one device no tile is named more than 2 times, a bound that some block reaches; every tile is named by some entry.
All inputs are finite; a program needn't handle non-finite values.
Results may differ from a plain program's by a relative error of at most 0.0049.
Values may be sent and summed in bfloat16 or wider, within the bound.
A program may use at most 64 MiB of HBM per device.

v0:
```python
import jax
import jax.numpy as jnp
from jax import lax
from jax.sharding import PartitionSpec as P

DATES = 32
TERMS = 7


highest = lax.Precision.HIGHEST


def harmonic_table(length):
    angles = 2.0 * jnp.pi * jnp.arange(length, dtype=jnp.float32) / length
    columns = [jnp.ones_like(angles)]
    for degree in range(1, 4):
        columns.append(jnp.cos(degree * angles))
        columns.append(jnp.sin(degree * angles))
    return jnp.stack(columns, axis=1)


def slot_predictions(coeffs, date_onehot, harmonic):
    date_table = jnp.dot(harmonic, coeffs, precision=highest)
    return jnp.dot(date_onehot.T, date_table, precision=highest)


def fit_tile(flattened, date_onehot, factor, harmonic):
    observed = jnp.dot(
        date_onehot.astype(jnp.bfloat16), flattened, preferred_element_type=jnp.float32
    )
    moments = jnp.dot(harmonic.T, observed, precision=highest)
    coeffs = jax.scipy.linalg.cho_solve((factor, True), moments)
    predicted = slot_predictions(coeffs, date_onehot, harmonic).astype(jnp.bfloat16)
    return (coeffs, predicted)


def date_tables(stamps, harmonic):
    matches = jnp.arange(DATES, dtype=jnp.int32)[:, None] == stamps[None, :]
    date_onehot = matches.astype(jnp.float32)
    tallies = jnp.sum(date_onehot, axis=1)
    normal = jnp.dot(harmonic.T, tallies[:, None] * harmonic, precision=highest) + jnp.eye(
        harmonic.shape[1], dtype=jnp.float32
    )
    return (date_onehot, jnp.linalg.cholesky(normal))


def on_device(blocks, row_maps, col_maps, targets, date_index):
    devices = lax.axis_size("dev")
    pieces = blocks.shape[0]
    width = blocks.shape[1]
    capacity = max(2, 4 * pieces // devices)
    slot_total = devices * capacity
    harmonic = harmonic_table(DATES)
    half_step = jnp.einsum(
        "pij,pkj->pik", blocks, col_maps, preferred_element_type=jnp.float32
    ).astype(jnp.bfloat16)
    resampled = jnp.einsum(
        "pij,pjk->pik", row_maps, half_step, preferred_element_type=jnp.float32
    ).astype(jnp.bfloat16)
    tile_ids = targets[:, 0]
    tile_onehot = (tile_ids[:, None] == jnp.arange(devices, dtype=jnp.int32)[None, :]).astype(
        jnp.int32
    )
    earlier = jnp.cumsum(tile_onehot, axis=0) - tile_onehot
    ranking = jnp.sum(earlier * tile_onehot, axis=1)
    slot_of = tile_ids * capacity + ranking
    outgoing = jnp.zeros((slot_total, width, width), jnp.bfloat16).at[slot_of].set(resampled)
    stamp_out = jnp.full((slot_total,), -1, jnp.int32).at[slot_of].set(date_index)
    received, stamps = (
        lax.all_to_all(outgoing, "dev", split_axis=0, concat_axis=0, tiled=True),
        lax.all_to_all(stamp_out, "dev", split_axis=0, concat_axis=0, tiled=True),
    )
    date_onehot, factor = date_tables(stamps, harmonic)
    coeffs, predicted = fit_tile(
        received.reshape(slot_total, width * width), date_onehot, factor, harmonic
    )
    returned_all = lax.all_to_all(
        predicted.reshape(slot_total, width, width), "dev", split_axis=0, concat_axis=0, tiled=True
    )
    coefficients = coeffs.reshape(TERMS, width, width)
    predicted_own = returned_all[slot_of]
    back_step = jnp.einsum(
        "pij,pjk->pik", predicted_own, col_maps, preferred_element_type=jnp.float32
    ).astype(jnp.bfloat16)
    adjoint = jnp.einsum("pji,pjk->pik", row_maps, back_step, preferred_element_type=jnp.float32)
    residuals = (blocks.astype(jnp.float32) - adjoint).astype(jnp.bfloat16)
    return (coefficients, residuals)


def solution(mesh):
    placed = (
        P("dev", None, None),
        P("dev", None, None),
        P("dev", None, None),
        P("dev", None),
        P("dev"),
    )
    return jax.shard_map(
        on_device,
        mesh=mesh,
        in_specs=placed,
        out_specs=(P("dev", None, None), P("dev", None, None)),
        check_vma=False,
    )
```

profile of v0, /device:TPU:1, one launch (start us, length us, event | category | flops | bytes accessed | tf_op | source)
XLA Modules:
  0.0 309.1 jit_solution(2821803875967056200)
XLA Ops:
  0.6 0.0 copy-start
  0.6 0.9 fusion.14
  1.5 0.1 reduce_window_sum.11
  1.6 0.8 select_reduce_fusion
  2.5 0.7 fusion.27
  3.1 0.9 scatter_custom_fusion
  4.0 0.8 all_to_all.12
  4.8 11.5 %all-to-all-start = ((s32[128,2,1]{1,2,0:T(1,128)}), s32[128,2,1]{1,2,0:T(1,128)S(1)}, u32[]{:S(2)}, u32[]{:S(2)}) async-start(s32[128,2,1]{1,2,0:T(1,128)} %bitcast.3), calls=%async_computation | async-start | bytes 131072 | tf_op jit(solution)/shard_map/all_to_all | solution.py:71
  16.3 0.0 copy-done
  16.3 6.6 %convert_bitcast_fusion = bf16[64,128,128]{1,2,0:T(8,128)(2,1)} fusion(bf16[64,128,128]{2,1,0:T(8,128)(2,1)S(1)} %copy-done, bf16[64,128,128]{2,1,0:T(8,128)(2,1)} %param.5, bf16[64,128,128]{2,1,0:T(8,128)(2,1)} %param.7), kind=kOutput, calls=%fused_computation.12 | convolution fusion | flops 538968064 | bytes 8388608 | tf_op jit(solution)/shard_map/pij,pjk->pik/dot_general | solution.py:57
  22.9 4.1 %copy.29 = bf16[64,128,128]{2,1,0:T(8,128)(2,1)} copy(bf16[64,128,128]{1,2,0:T(8,128)(2,1)} %convert_bitcast_fusion) | data formatting | bytes 4194304 | tf_op jit(solution)/shard_map/convert_element_type | solution.py:59
  26.9 5.3 %broadcast_in_dim.6 = bf16[256,128,128]{2,1,0:T(8,128)(2,1)} broadcast(bf16[]{:T(256)} %constant.77.clone.1), dimensions={} | broadcast | bytes 8388610 | tf_op jit(solution)/shard_map/broadcast_in_dim | solution.py:67
  32.3 10.0 %scatter_fusion = bf16[256,128,128]{2,1,0:T(8,128)(2,1)} fusion(bf16[256,128,128]{2,1,0:T(8,128)(2,1)} %broadcast_in_dim.6, s32[64]{0:T(128)S(1)} %fusion.27, bf16[64,128,128]{2,1,0:T(8,128)(2,1)} %copy.29), kind=kCustom, calls=%fused_computation.2 | custom fusion | bytes 6291712 | tf_op jit(solution)/shard_map/scatter | solution.py:67
  42.3 0.0 all-to-all-done
  42.3 10.2 %all-to-all-start.1 = ((bf16[256,128,128]{2,1,0:T(8,128)(2,1)}), bf16[256,128,128]{2,1,0:T(8,128)(2,1)}, u32[]{:S(2)}, u32[]{:S(2)}) async-start(bf16[256,128,128]{2,1,0:T(8,128)(2,1)} %scatter_fusion), calls=%async_computation.1 | async-start | bytes 16777216 | tf_op jit(solution)/shard_map/all_to_all | solution.py:70
  52.6 0.5 broadcast.140
  53.2 0.8 reduce.9
  54.0 0.1 eq.39
  54.1 0.1 convert_reduce_fusion
  54.2 0.1 fusion.17
  54.4 0.1 copy.26
  54.5 0.6 cholesky.17
  55.1 0.1 select_reduce_fusion.1
  55.1 0.6 compare_reduce_fusion
  55.8 0.6 fusion.19
  56.4 0.5 custom-call.10
  57.0 94.2 %all-to-all-done.1 = bf16[256,128,128]{2,1,0:T(8,128)(2,1)} async-done(((bf16[256,128,128]{2,1,0:T(8,128)(2,1)}), bf16[256,128,128]{2,1,0:T(8,128)(2,1)}, u32[]{:S(2)}, u32[]{:S(2)}) %all-to-all-start.1) | async-done | bytes 8388640 | tf_op jit(solution)/shard_map/all_to_all | solution.py:70
  151.2 8.2 %fusion = f32[32,16384]{1,0:T(8,128)S(1)} fusion(bf16[32,8,128,128]{3,2,1,0:T(8,128)(2,1)} %bitcast.11, s32[256]{0:T(256)S(1)} %eq.39), kind=kOutput, calls=%fused_computation.4 | convolution fusion | flops 268460032 | bytes 10486784 | tf_op jit(solution)/shard_map/dot_general | solution.py:28
  159.3 1.1 fusion.36
  160.5 0.7 fusion.20
  161.1 0.6 fusion.22
  161.7 1.9 fusion.37
  163.6 9.2 %fusion.3 = bf16[32,8,128,128]{3,1,2,0:T(8,128)(2,1)} fusion(f32[32,16384]{1,0:T(8,128)S(1)} %fusion.37, s32[256]{0:T(256)S(1)} %eq.39), kind=kOutput, calls=%fused_computation.7 | convolution fusion | flops 1614815232 | bytes 10486784 | tf_op jit(solution)/shard_map/dot_general | solution.py:24
  172.8 9.2 %copy.37 = bf16[32,8,128,128]{3,2,1,0:T(8,128)(2,1)} copy(bf16[32,8,128,128]{3,1,2,0:T(8,128)(2,1)} %fusion.3) | data formatting | bytes 16777216
  182.0 13.2 %all-to-all-start.2 = ((bf16[256,128,128]{2,1,0:T(8,128)(2,1)}), bf16[256,128,128]{2,1,0:T(8,128)(2,1)}, u32[]{:S(2)}, u32[]{:S(2)}) async-start(bf16[256,128,128]{2,1,0:T(8,128)(2,1)} %bitcast.55), calls=%async_computation.2 | async-start | bytes 16777216 | tf_op jit(solution)/shard_map/all_to_all | solution.py:77
  195.2 4.1 %copy.30 = bf16[64,128,128]{1,2,0:T(8,128)(2,1)} copy(bf16[64,128,128]{2,1,0:T(8,128)(2,1)} %param.5) | data formatting | bytes 4194304 | tf_op args[0]
  199.3 0.9 copy.43
  200.1 93.7 %all-to-all-done.2 = bf16[256,128,128]{2,1,0:T(8,128)(2,1)} async-done(((bf16[256,128,128]{2,1,0:T(8,128)(2,1)}), bf16[256,128,128]{2,1,0:T(8,128)(2,1)}, u32[]{:S(2)}, u32[]{:S(2)}) %all-to-all-start.2) | async-done | bytes 8388640 | tf_op jit(solution)/shard_map/all_to_all | solution.py:77
  293.9 5.6 %gather_fusion = bf16[64,128,128]{2,1,0:T(8,128)(2,1)} fusion(bf16[256,128,128]{2,1,0:T(8,128)(2,1)} %all-to-all-done.2, s32[1024]{0:T(1024)S(1)} %pad_clamp_fusion), kind=kCustom, calls=%fused_computation | custom fusion | bytes 4194560 | tf_op jit(solution)/shard_map/gather | solution.py:81
  299.4 5.5 %fusion.4 = bf16[64,128,128]{1,2,0:T(8,128)(2,1)} fusion(bf16[64,128,128]{1,2,0:T(8,128)(2,1)} %copy.30, bf16[64,128,128]{2,1,0:T(8,128)(2,1)S(1)} %copy-done, bf16[64,128,128]{2,1,0:T(8,128)(2,1)} %gather_fusion, bf16[64,128,128]{2,1,0:T(8,128)(2,1)} %param.7), kind=kOutput, calls=%fused_computation.9 | convolution fusion | flops 541065216 | bytes 10485760 | tf_op jit(solution)/shard_map/pji,pjk->pik/dot_general | solution.py:85
  305.0 4.1 %copy.32 = bf16[64,128,128]{2,1,0:T(8,128)(2,1)} copy(bf16[64,128,128]{1,2,0:T(8,128)(2,1)} %fusion.4) | data formatting | bytes 4194304
  (7 shorter events, 0.2 us)
Async XLA Ops:
  0.6 15.7 %copy-start = (bf16[64,128,128]{2,1,0:T(8,128)(2,1)S(1)}, bf16[64,128,128]{2,1,0:T(8,128)(2,1)}, u32[]{:S(2)}) copy-start(bf16[64,128,128]{2,1,0:T(8,128)(2,1)} %param.6) | copy-start | bytes 6291460
  4.8 37.5 %all-to-all-start = ((s32[128,2,1]{1,2,0:T(1,128)}), s32[128,2,1]{1,2,0:T(1,128)S(1)}, u32[]{:S(2)}, u32[]{:S(2)}) async-start(s32[128,2,1]{1,2,0:T(1,128)} %bitcast.3), calls=%async_computation | async-start | bytes 131072 | tf_op jit(solution)/shard_map/all_to_all | solution.py:71
  42.3 108.9 %all-to-all-start.1 = ((bf16[256,128,128]{2,1,0:T(8,128)(2,1)}), bf16[256,128,128]{2,1,0:T(8,128)(2,1)}, u32[]{:S(2)}, u32[]{:S(2)}) async-start(bf16[256,128,128]{2,1,0:T(8,128)(2,1)} %scatter_fusion), calls=%async_computation.1 | async-start | bytes 16777216 | tf_op jit(solution)/shard_map/all_to_all | solution.py:70
  182.0 111.9 %all-to-all-start.2 = ((bf16[256,128,128]{2,1,0:T(8,128)(2,1)}), bf16[256,128,128]{2,1,0:T(8,128)(2,1)}, u32[]{:S(2)}, u32[]{:S(2)}) async-start(bf16[256,128,128]{2,1,0:T(8,128)(2,1)} %bitcast.55), calls=%async_computation.2 | async-start | bytes 16777216 | tf_op jit(solution)/shard_map/all_to_all | solution.py:77
where the time goes:
time: 313 us; the launch traced here: 309 us
  waiting for transfers between devices  188 us (60%)
  local copies, waits for them, and re-layouts  45.6 us (15%)
  starting transfers between devices  34.8 us (11%)
  matrix products  33.8 us (11%)
  other arithmetic  6.06 us (2%)
    all_to_all x1, waiting for transfers between devices, on_device(): lax.all_to_all(outgoing, 'dev', split_axis=0, concat_axis=0, tiled=True)  94.2 us
    all_to_all x1, waiting for transfers between devices, on_device(): lax.all_to_all(predicted.reshape(slot_total, width, width), 'dev', split_...  93.7 us
    unnamed x6, local copies, waits for them, and re-layouts  18.2 us
    all_to_all x1, starting transfers between devices, on_device(): lax.all_to_all(predicted.reshape(slot_total, width, width), 'dev', split_...  13.2 us
    all_to_all x1, starting transfers between devices, on_device(): lax.all_to_all(stamp_out, 'dev', split_axis=0, concat_axis=0, tiled=True)  11.5 us
    all_to_all x1, starting transfers between devices, on_device(): lax.all_to_all(outgoing, 'dev', split_axis=0, concat_axis=0, tiled=True)  10.2 us
    scatter x1, local copies, waits for them, and re-layouts, on_device(): jnp.zeros((slot_total, width, width), jnp.bfloat16).at[slot_of]  10 us
    dot_general x1, matrix products, slot_predictions(): return jnp.dot(date_onehot.T, date_table, precision=highest)  9.22 us
  transfers between devices with their start and end apart: 3, of which 2 were waited for; matrix products, arithmetic and copies ran while one was open for 11% of the time, Pallas kernels for 0%

commit v1 on v0

v1 whole, which is shorter than its diff:
```python
import functools

import jax
import jax.numpy as jnp
import numpy as np
from jax import lax
from jax.experimental import pallas as pl
from jax.experimental.pallas import tpu as pltpu
from jax.sharding import PartitionSpec as P

N = 128
DATES = 32
TERMS = 7
BLK = 128
UNIT = 16
UNITS = 4
PAIR = 256
LOW = 16
CHUNKS = ((0, 1), (1, 2), (3, 1))
MESH = pl.DeviceIdType.MESH
f32 = jnp.float32
bf16 = jnp.bfloat16
highest = lax.Precision.HIGHEST
PAIRS = [(k, l) for k in range(TERMS) for l in range(k + 1)]


def harmonic_table():
    angles = 2.0 * np.pi * np.arange(DATES) / DATES
    columns = [np.ones(DATES)]
    for degree in range(1, 4):
        columns.append(np.cos(degree * angles))
        columns.append(np.sin(degree * angles))
    return np.stack(columns, axis=1)


def iota(shape, dim):
    return lax.broadcasted_iota(jnp.int32, shape, dim)


def inverse_rows(normal):
    low = {}
    for j in range(TERMS):
        for i in range(j, TERMS):
            s = normal[i, j]
            for m in range(j):
                s = s - low[i, m] * low[j, m]
            if i == j:
                root = jnp.sqrt(s)
                low[j, j] = root
                low[j, "inv"] = 1.0 / root
            else:
                low[i, j] = s * low[j, "inv"]
    inv = {}
    for j in range(TERMS):
        inv[j, j] = low[j, "inv"]
        for i in range(j + 1, TERMS):
            s = low[i, j] * inv[j, j]
            for m in range(j + 1, i):
                s = s + low[i, m] * inv[m, j]
            inv[i, j] = -s * low[i, "inv"]
    out = []
    for k, l in PAIRS:
        s = inv[k, k] * inv[k, l]
        for m in range(k + 1, TERMS):
            s = s + inv[m, k] * inv[m, l]
        out.append(s)
    return out


def kernel(
    b_hbm, r_hbm, c_hbm, t_ref, d_ref, table_ref, products_ref,
    coef_hbm, res_hbm,
    bv, rv, cv, meta_own, meta, send1, recv1, send2, recv2, w, wt, tmp,
    trow, drow, tally, inv_rows, inv_full, moments, coefs, coef_send, coef_recv, ctmp, coef_out,
    load_sem, stage_sem, meta_ss, meta_rs, ss1, rs1, ss2, rs2, coef_ss, coef_rs, own_sem, out_sem,
):
    me = lax.axis_index("dev")
    loads = []
    for u in range(UNITS):
        part = pl.ds(u * UNIT, UNIT)
        loads.append([
            pltpu.make_async_copy(src.at[part], dst.at[part], load_sem.at[i, u])
            for i, (src, dst) in enumerate(((b_hbm, bv), (c_hbm, cv), (r_hbm, rv)))
        ])
    for group in loads:
        for copy in group:
            copy.start()

    barrier = pltpu.get_barrier_semaphore()
    base = (me // LOW) * LOW

    @pl.loop(1, LOW)
    def _(i):
        peer = base + lax.rem(me + i, LOW)
        pl.semaphore_signal(barrier, inc=1, device_id=(peer,), device_id_type=MESH)

    @pl.loop(1, N // LOW)
    def _(i):
        peer = lax.rem(me + i * LOW, N)
        pl.semaphore_signal(barrier, inc=1, device_id=(peer,), device_id_type=MESH)

    def resample(u):
        for copy in loads[u]:
            copy.wait()
        for e in range(UNIT):
            p = u * UNIT + e
            half = lax.dot_general(
                bv[p], cv[p], (((1,), (1,)), ((), ())), preferred_element_type=f32
            ).astype(bf16)
            tmp[pl.ds(e, BLK, stride=UNIT), :] = jnp.dot(rv[p], half, preferred_element_type=f32)

        @pl.loop(0, 8)
        def _(i):
            rows = tmp[pl.ds(pl.multiple_of(i * 256, 256), 256), :]
            send1[u, pl.ds(i * 16, 16)] = rows.astype(bf16).reshape(16, UNIT, BLK)

    def exchange(src, dst, ss, rs, first, count, lane):
        units = pl.ds(first, count)
        own = pltpu.make_async_copy(src.at[units, me], dst.at[units, me], own_sem.at[lane])
        own.start()

        @pl.loop(1, N)
        def _(i):
            peer = lax.rem(me + i, N)
            pltpu.make_async_remote_copy(
                src_ref=src.at[units, peer], dst_ref=dst.at[units, me],
                send_sem=ss, recv_sem=rs, device_id=(peer,), device_id_type=MESH,
            ).start()

        return own

    def settle(ref, sem, first, count):
        part = ref.at[pl.ds(first, count), pl.ds(0, N - 1)]
        pltpu.make_async_copy(part, part, sem).wait()

    meta_own[0:1, 0:64] = t_ref[...]
    meta_own[0:1, 64:128] = d_ref[...]
    resample(0)
    pl.semaphore_wait(barrier, LOW - 1 + N // LOW - 1)

    @pl.loop(1, N // LOW)
    def _(i):
        peer = lax.rem(me + i * LOW, N)
        pl.semaphore_signal(stage_sem, inc=1, device_id=(peer,), device_id_type=MESH)

    pl.semaphore_wait(stage_sem, N // LOW - 1)

    own_meta = pltpu.make_async_copy(meta_own, meta.at[me], own_sem.at[6])
    own_meta.start()

    @pl.loop(1, N)
    def _(i):
        peer = lax.rem(me + i, N)
        pltpu.make_async_remote_copy(
            src_ref=meta_own, dst_ref=meta.at[me],
            send_sem=meta_ss, recv_sem=meta_rs, device_id=(peer,), device_id_type=MESH,
        ).start()

    owns1 = []
    for c, (first, count) in enumerate(CHUNKS):
        for u in range(first, first + count):
            if u > 0:
                resample(u)
        owns1.append(exchange(send1, recv1, ss1.at[c], rs1.at[c], first, count, c))

    part = meta.at[pl.ds(0, N - 1)]
    pltpu.make_async_copy(part, part, meta_rs).wait()
    own_meta.wait()
    names = meta[:, 0, :].astype(f32).astype(bf16)
    lane_in, lane_out = iota((N, PAIR), 0), iota((N, PAIR), 1)
    mine = (lane_out // UNIT) == lax.rem(lane_in, 16)
    gather = (iota((8, N), 0) == iota((8, N), 1) // 16).astype(f32).astype(bf16)
    for u in range(UNITS):
        for start, out in ((0, trow), (64, drow)):
            pick = (lane_in == start + u * UNIT + lax.rem(lane_out, UNIT)).astype(f32).astype(bf16)
            spread = jnp.dot(names, pick, preferred_element_type=f32)
            spread = jnp.where(mine, spread, 0.0).astype(bf16)
            out[pl.ds(u * 8, 8), :] = jnp.dot(gather, spread, preferred_element_type=f32)

    tally[...] = jnp.zeros_like(tally)
    table = table_ref[...].astype(bf16)

    @pl.loop(0, UNITS)
    def _(u):
        @pl.loop(0, 8)
        def _(g):
            pair = u * 8 + g
            tile = trow[pl.ds(pair, 1), :]
            date = drow[pl.ds(pair, 1), :]
            tile_hot = (iota((N, PAIR), 0).astype(f32) == tile).astype(f32).astype(bf16)
            date_hot = (iota((DATES, PAIR), 0).astype(f32) == date).astype(f32).astype(bf16)
            tally[...] += lax.dot_general(
                date_hot, tile_hot, (((1,), (1,)), ((), ())), preferred_element_type=f32
            )
            weights = jnp.dot(table, date_hot, preferred_element_type=f32)
            lanes = pl.ds(pl.multiple_of(g * PAIR, PAIR), PAIR)
            for k in range(TERMS):
                w[u, pl.ds(k * N, N), lanes] = tile_hot * weights[k : k + 1, :].astype(bf16)
            columns = jnp.where(iota((8, PAIR), 0) == 7, tile, weights).T
            hit = iota((PAIR, N), 1).astype(f32) == columns[:, 7:8]
            for k in range(TERMS):
                wt[pair, :, pl.ds(k * N, N)] = jnp.where(hit, columns[:, k : k + 1], 0.0).astype(bf16)

    normal_rows = jnp.dot(products_ref[...], tally[...], precision=highest, preferred_element_type=f32)
    normal = {}
    for i, (k, l) in enumerate(PAIRS):
        row = normal_rows[i : i + 1, :]
        normal[k, l] = row + 1.0 if k == l else row
    inv_rows[...] = jnp.zeros_like(inv_rows)
    for i, row in enumerate(inverse_rows(normal)):
        inv_rows[i : i + 1, :] = row
    columns = inv_rows[...].T
    for i in range(len(PAIRS)):
        inv_full[i] = jnp.broadcast_to(columns[:, i : i + 1], (N, BLK))

    @pl.loop(0, UNITS * UNIT)
    def _(p):
        rv[p] = rv[p].T

    for c, (first, count) in enumerate(CHUNKS):
        settle(recv1, rs1.at[c], first, count)
        owns1[c].wait()
        for u in range(first, first + count):
            part = jnp.dot(
                w[u], recv1[u].reshape(N * UNIT, BLK), preferred_element_type=f32
            )
            if u == 0:
                moments[...] = part
            else:
                moments[...] += part

    at = {}
    for i, (k, l) in enumerate(PAIRS):
        at[k, l] = at[l, k] = i

    @pl.loop(0, N // 16)
    def _(i):
        rows = pl.multiple_of(i * 16, 16)
        given = [moments[pl.ds(l * N + rows, 16), :] for l in range(TERMS)]
        for k in range(TERMS):
            value = inv_full[at[k, 0], pl.ds(rows, 16), :] * given[0]
            for l in range(1, TERMS):
                value = value + inv_full[at[k, l], pl.ds(rows, 16), :] * given[l]
            coefs[pl.ds(k * N + rows, 16), :] = value.astype(bf16)
            ctmp[pl.ds(rows * 8 + k, 16, stride=8), :] = value
        ctmp[pl.ds(rows * 8 + 7, 16, stride=8), :] = jnp.zeros((16, BLK), f32)
        coef_send[pl.ds(rows, 16)] = (
            ctmp[pl.ds(rows * 8, 128), :].astype(bf16).reshape(16, 8, BLK)
        )

    own_coef = pltpu.make_async_copy(coef_send.at[me], coef_recv.at[me], own_sem.at[7])
    own_coef.start()

    @pl.loop(1, N)
    def _(i):
        peer = lax.rem(me + i, N)
        pltpu.make_async_remote_copy(
            src_ref=coef_send.at[peer], dst_ref=coef_recv.at[me],
            send_sem=coef_ss, recv_sem=coef_rs, device_id=(peer,), device_id_type=MESH,
        ).start()

    def predict(u):
        @pl.loop(0, 2)
        def _(i):
            rows = wt[pl.ds(u * 8 + i * 4, 4)].reshape(4 * PAIR, TERMS * N)
            value = jnp.dot(rows, coefs[...], preferred_element_type=f32)
            send2[u, pl.ds(i * 64, 64)] = value.astype(bf16).reshape(64, UNIT, BLK)

    owns2 = []
    for c, (first, count) in enumerate(CHUNKS):
        for u in range(first, first + count):
            predict(u)
        owns2.append(exchange(send2, recv2, ss2.at[c], rs2.at[c], first, count, 3 + c))

    part = coef_recv.at[pl.ds(0, N - 1)]
    pltpu.make_async_copy(part, part, coef_rs).wait()
    own_coef.wait()
    ctmp[...] = coef_recv[...].astype(f32).reshape(N * 8, BLK)
    for k in range(TERMS):
        coef_out[k] = ctmp[pl.ds(k, N, stride=8), :]
    outs = [pltpu.make_async_copy(coef_out, coef_hbm, out_sem.at[UNITS])]
    outs[0].start()

    for c, (first, count) in enumerate(CHUNKS):
        settle(recv2, rs2.at[c], first, count)
        owns2[c].wait()
        for u in range(first, first + count):
            @pl.loop(0, 8)
            def _(i):
                rows = recv2[u, pl.ds(i * 16, 16)].astype(f32).reshape(256, BLK)
                tmp[pl.ds(pl.multiple_of(i * 256, 256), 256), :] = rows

            for e in range(UNIT):
                p = u * UNIT + e
                predicted = tmp[pl.ds(e, BLK, stride=UNIT), :].astype(bf16)
                back = jnp.dot(predicted, cv[p], preferred_element_type=f32).astype(bf16)
                adjoint = jnp.dot(rv[p], back, preferred_element_type=f32)
                bv[p] = (bv[p].astype(f32) - adjoint).astype(bf16)
            part = pl.ds(u * UNIT, UNIT)
            outs.append(pltpu.make_async_copy(bv.at[part], res_hbm.at[part], out_sem.at[u]))
            outs[-1].start()

    part = meta.at[pl.ds(0, N - 1)]
    pltpu.make_async_copy(part, part, meta_ss).wait()
    part = coef_send.at[pl.ds(0, N - 1)]
    pltpu.make_async_copy(part, part, coef_ss).wait()
    for c, (first, count) in enumerate(CHUNKS):
        settle(send1, ss1.at[c], first, count)
        settle(send2, ss2.at[c], first, count)
    for copy in outs:
        copy.wait()


def on_device(blocks, row_maps, col_maps, targets, date_index):
    entries = UNITS * UNIT
    harmonic = harmonic_table()
    table = np.zeros((8, DATES), np.float32)
    table[:TERMS] = harmonic.T
    products = np.zeros((32, DATES), np.float32)
    for i, (k, l) in enumerate(PAIRS):
        products[i] = harmonic[:, k] * harmonic[:, l]
    dma = pltpu.SemaphoreType.DMA
    chunks = len(CHUNKS)
    vmem = pl.BlockSpec(memory_space=pltpu.VMEM)
    hbm = pl.BlockSpec(memory_space=pl.ANY)
    return pl.pallas_call(
        kernel,
        out_shape=(
            jax.ShapeDtypeStruct((TERMS, BLK, BLK), f32),
            jax.ShapeDtypeStruct((entries, BLK, BLK), bf16),
        ),
        in_specs=[hbm] * 3 + [vmem] * 4,
        out_specs=(hbm, hbm),
        scratch_shapes=[
            pltpu.VMEM((entries, BLK, BLK), bf16),
            pltpu.VMEM((entries, BLK, BLK), bf16),
            pltpu.VMEM((entries, BLK, BLK), bf16),
            pltpu.VMEM((1, 128), jnp.int32),
            pltpu.VMEM((N, 1, 128), jnp.int32),
            pltpu.VMEM((UNITS, N, UNIT, BLK), bf16),
            pltpu.VMEM((UNITS, N, UNIT, BLK), bf16),
            pltpu.VMEM((UNITS, N, UNIT, BLK), bf16),
            pltpu.VMEM((UNITS, N, UNIT, BLK), bf16),
            pltpu.VMEM((UNITS, TERMS * N, N * UNIT), bf16),
            pltpu.VMEM((UNITS * 8, PAIR, TERMS * N), bf16),
            pltpu.VMEM((N * UNIT, BLK), f32),
            pltpu.VMEM((UNITS * 8, PAIR), f32),
            pltpu.VMEM((UNITS * 8, PAIR), f32),
            pltpu.VMEM((DATES, N), f32),
            pltpu.VMEM((32, N), f32),
            pltpu.VMEM((len(PAIRS), N, BLK), f32),
            pltpu.VMEM((TERMS * N, BLK), f32),
            pltpu.VMEM((TERMS * N, BLK), bf16),
            pltpu.VMEM((N, 8, BLK), bf16),
            pltpu.VMEM((N, 8, BLK), bf16),
            pltpu.VMEM((N * 8, BLK), f32),
            pltpu.VMEM((TERMS, N, BLK), f32),
            dma((3, UNITS)),
            pltpu.SemaphoreType.REGULAR,
            dma,
            dma,
            dma((chunks,)),
            dma((chunks,)),
            dma((chunks,)),
            dma((chunks,)),
            dma,
            dma,
            dma((8,)),
            dma((UNITS + 1,)),
        ],
        compiler_params=pltpu.CompilerParams(
            collective_id=0, has_side_effects=True, vmem_limit_bytes=58 * 2**20
        ),
        name="fit",
    )(
        blocks, row_maps, col_maps, targets.reshape(1, entries), date_index.reshape(1, entries),
        jnp.asarray(table), jnp.asarray(products),
    )


def solution(mesh):
    placed = (
        P("dev", None, None),
        P("dev", None, None),
        P("dev", None, None),
        P("dev", None),
        P("dev"),
    )
    return jax.shard_map(
        on_device,
        mesh=mesh,
        in_specs=placed,
        out_specs=(P("dev", None, None), P("dev", None, None)),
        check_vma=False,
    )
```

time: 313 us -> 95.9 us (0.31); the launches traced: 309 us -> 95.6 us
  waiting for transfers between devices: 188 us -> 0 us
  Pallas kernels: 0 us -> 90 us
  local copies, waits for them, and re-layouts: 45.6 us -> 4.97 us
  starting transfers between devices: 34.8 us -> 0 us
  matrix products: 33.8 us -> 0 us
  other arithmetic: 6.06 us -> 0 us
    all_to_all x3 -> x0, waiting for transfers between devices: 188 us -> none  [the longest x1 94.2 us: on_device(): lax.all_to_all(outgoing, 'dev', split_axis=0, concat_axis=0, tiled=True)]
    pallas_call x0 -> x1, Pallas kernels: none -> 90 us  [on_device(): pl.pallas_call(kernel, out_shape=(jax.ShapeDtypeStruct((TERMS, BLK, BLK),...]
    all_to_all x3 -> x0, starting transfers between devices: 34.8 us -> none  [the longest x1 13.2 us: on_device(): lax.all_to_all(predicted.reshape(slot_total, width, width), 'dev', split_...]
    dot_general x7 -> x0, matrix products: 32.6 us -> none  [the longest x1 9.22 us: slot_predictions(): return jnp.dot(date_onehot.T, date_table, precision=highest)]
    unnamed x6 -> x2, local copies, waits for them, and re-layouts: 18.2 us -> 4.97 us
    scatter x2 -> x0, local copies, waits for them, and re-layouts: 10.9 us -> none  [the longest x1 10 us: on_device(): jnp.zeros((slot_total, width, width), jnp.bfloat16).at[slot_of]]
    gather x1 -> x0, local copies, waits for them, and re-layouts: 5.59 us -> none  [on_device(): predicted_own = returned_all[slot_of]]
    broadcast_in_dim x1 -> x0, local copies, waits for them, and re-layouts: 5.34 us -> none  [on_device(): jnp.zeros((slot_total, width, width), jnp.bfloat16).at[slot_of]]
  transfers between devices with their start and end apart: 3 -> 0, of which waited for: 2 -> 0; matrix products, arithmetic and copies ran while one was open for 11% -> 0% of each run, Pallas kernels for 0% -> 0%
where the time goes in v1:
time: 95.9 us; the launch traced here: 95.6 us
  Pallas kernels  90 us (94%)
  local copies, waits for them, and re-layouts  4.97 us (5%)
    pallas_call x1, Pallas kernels, on_device(): pl.pallas_call(kernel, out_shape=(jax.ShapeDtypeStruct((TERMS, BLK, BLK),...  90 us
    unnamed x2, local copies, waits for them, and re-layouts  4.97 us

profile of v1, /device:TPU:1, one launch (start us, length us, event | category | flops | bytes accessed | tf_op | source)
XLA Modules:
  0.0 95.6 jit_solution(13117812227372766942)
XLA Ops:
  0.6 90.0 %fit.1 = (f32[7,128,128]{2,1,0:T(8,128)}, bf16[64,128,128]{2,1,0:T(8,128)(2,1)}) custom-call(bf16[64,128,128]{2,1,0:T(8,128)(2,1)} %b_hbm.1, bf16[64,128,128]{2,1,0:T(8,128)(2,1)} %r_hbm.1, bf16[64,128,128]{2,1,0:T(8,128)(2,1)} %c_hbm.1, s32[1,64]{1,0:T(1,128)} %bitcast.2, s32[1,64]{1,0:T(1,128)} %bitcast.3, f32[8,32]{1,0:T(8,128)} %constant.4.clone.table_ref, ...), custom_call_target="tpu_custom_call" | custom-call | tf_op jit(solution)/shard_map/fit/pallas_call | solution.py:326
  90.6 1.8 %copy.11 = f32[7,128,128]{2,1,0:T(8,128)} copy(f32[7,128,128]{2,1,0:T(8,128)} %get-tuple-element.4) | data formatting | bytes 917504
  92.4 3.2 %copy.12 = bf16[64,128,128]{2,1,0:T(8,128)(2,1)} copy(bf16[64,128,128]{2,1,0:T(8,128)(2,1)} %get-tuple-element.5) | data formatting | bytes 4194304

commit v2 on v1

--- a/solution.py
+++ b/solution.py
@@ -16,6 +16,7 @@
 UNITS = 4
 PAIR = 256
 LOW = 16
+MOVES = 8
 CHUNKS = ((0, 1), (1, 2), (3, 1))
 MESH = pl.DeviceIdType.MESH
 f32 = jnp.float32
@@ -70,8 +71,8 @@
 def kernel(
     b_hbm, r_hbm, c_hbm, t_ref, d_ref, table_ref, products_ref,
     coef_hbm, res_hbm,
-    bv, rv, cv, meta_own, meta, send1, recv1, send2, recv2, w, wt, tmp,
-    trow, drow, tally, inv_rows, inv_full, moments, coefs, coef_send, coef_recv, ctmp, coef_out,
+    bv, rv, cv, meta_own, meta, send1, recv1, send2, recv2, w, tmp,
+    trow, drow, tally, inv_rows, inv_full, moments, coefs_t, coefs, coef_send, coef_recv, ctmp, coef_out,
     load_sem, stage_sem, meta_ss, meta_rs, ss1, rs1, ss2, rs2, coef_ss, coef_rs, own_sem, out_sem,
 ):
     me = lax.axis_index("dev")
@@ -119,9 +120,9 @@
         own = pltpu.make_async_copy(src.at[units, me], dst.at[units, me], own_sem.at[lane])
         own.start()
 
-        @pl.loop(1, N)
+        @pl.loop(1, N, unroll=4)
         def _(i):
-            peer = lax.rem(me + i, N)
+            peer = lax.rem(me + i * 37, N)
             pltpu.make_async_remote_copy(
                 src_ref=src.at[units, peer], dst_ref=dst.at[units, me],
                 send_sem=ss, recv_sem=rs, device_id=(peer,), device_id_type=MESH,
@@ -144,17 +145,6 @@
         pl.semaphore_signal(stage_sem, inc=1, device_id=(peer,), device_id_type=MESH)
 
     pl.semaphore_wait(stage_sem, N // LOW - 1)
-
-    own_meta = pltpu.make_async_copy(meta_own, meta.at[me], own_sem.at[6])
-    own_meta.start()
-
-    @pl.loop(1, N)
-    def _(i):
-        peer = lax.rem(me + i, N)
-        pltpu.make_async_remote_copy(
-            src_ref=meta_own, dst_ref=meta.at[me],
-            send_sem=meta_ss, recv_sem=meta_rs, device_id=(peer,), device_id_type=MESH,
-        ).start()
 
     owns1 = []
     for c, (first, count) in enumerate(CHUNKS):
@@ -162,6 +152,17 @@
             if u > 0:
                 resample(u)
         owns1.append(exchange(send1, recv1, ss1.at[c], rs1.at[c], first, count, c))
+        if c == 0:
+            own_meta = pltpu.make_async_copy(meta_own, meta.at[me], own_sem.at[6])
+            own_meta.start()
+
+            @pl.loop(1, N, unroll=4)
+            def _(i):
+                peer = lax.rem(me + i * 37, N)
+                pltpu.make_async_remote_copy(
+                    src_ref=meta_own, dst_ref=meta.at[me],
+                    send_sem=meta_ss, recv_sem=meta_rs, device_id=(peer,), device_id_type=MESH,
+                ).start()
 
     part = meta.at[pl.ds(0, N - 1)]
     pltpu.make_async_copy(part, part, meta_rs).wait()
@@ -196,10 +197,6 @@
             lanes = pl.ds(pl.multiple_of(g * PAIR, PAIR), PAIR)
             for k in range(TERMS):
                 w[u, pl.ds(k * N, N), lanes] = tile_hot * weights[k : k + 1, :].astype(bf16)
-            columns = jnp.where(iota((8, PAIR), 0) == 7, tile, weights).T
-            hit = iota((PAIR, N), 1).astype(f32) == columns[:, 7:8]
-            for k in range(TERMS):
-                wt[pair, :, pl.ds(k * N, N)] = jnp.where(hit, columns[:, k : k + 1], 0.0).astype(bf16)
 
     normal_rows = jnp.dot(products_ref[...], tally[...], precision=highest, preferred_element_type=f32)
     normal = {}
@@ -213,10 +210,6 @@
     for i in range(len(PAIRS)):
         inv_full[i] = jnp.broadcast_to(columns[:, i : i + 1], (N, BLK))
 
-    @pl.loop(0, UNITS * UNIT)
-    def _(p):
-        rv[p] = rv[p].T
-
     for c, (first, count) in enumerate(CHUNKS):
         settle(recv1, rs1.at[c], first, count)
         owns1[c].wait()
@@ -241,7 +234,7 @@
             value = inv_full[at[k, 0], pl.ds(rows, 16), :] * given[0]
             for l in range(1, TERMS):
                 value = value + inv_full[at[k, l], pl.ds(rows, 16), :] * given[l]
-            coefs[pl.ds(k * N + rows, 16), :] = value.astype(bf16)
+            coefs[k, pl.ds(rows, 16), :] = value.astype(bf16)
             ctmp[pl.ds(rows * 8 + k, 16, stride=8), :] = value
         ctmp[pl.ds(rows * 8 + 7, 16, stride=8), :] = jnp.zeros((16, BLK), f32)
         coef_send[pl.ds(rows, 16)] = (
@@ -251,26 +244,33 @@
     own_coef = pltpu.make_async_copy(coef_send.at[me], coef_recv.at[me], own_sem.at[7])
     own_coef.start()
 
-    @pl.loop(1, N)
+    @pl.loop(1, N, unroll=4)
     def _(i):
-        peer = lax.rem(me + i, N)
+        peer = lax.rem(me + i * 37, N)
         pltpu.make_async_remote_copy(
             src_ref=coef_send.at[peer], dst_ref=coef_recv.at[me],
             send_sem=coef_ss, recv_sem=coef_rs, device_id=(peer,), device_id_type=MESH,
         ).start()
 
+    for k in range(TERMS):
+        coefs_t[:, k * N : (k + 1) * N] = coefs[k].T
+
     def predict(u):
-        @pl.loop(0, 2)
+        @pl.loop(0, 4)
         def _(i):
-            rows = wt[pl.ds(u * 8 + i * 4, 4)].reshape(4 * PAIR, TERMS * N)
-            value = jnp.dot(rows, coefs[...], preferred_element_type=f32)
-            send2[u, pl.ds(i * 64, 64)] = value.astype(bf16).reshape(64, UNIT, BLK)
+            lanes = pl.ds(pl.multiple_of(i * 512, 512), 512)
+            value = jnp.dot(coefs_t[...], w[u, :, lanes], preferred_element_type=f32)
+            send2[u, pl.ds(i * 32, 32)] = value.astype(bf16).T.reshape(32, UNIT, BLK)
 
     owns2 = []
     for c, (first, count) in enumerate(CHUNKS):
         for u in range(first, first + count):
             predict(u)
         owns2.append(exchange(send2, recv2, ss2.at[c], rs2.at[c], first, count, 3 + c))
+
+    @pl.loop(0, UNITS * UNIT, unroll=4)
+    def _(p):
+        rv[p] = rv[p].T
 
     part = coef_recv.at[pl.ds(0, N - 1)]
     pltpu.make_async_copy(part, part, coef_rs).wait()
@@ -308,6 +308,22 @@
         settle(send1, ss1.at[c], first, count)
         settle(send2, ss2.at[c], first, count)
     for copy in outs:
+        copy.wait()
+
+
+def move(coef, res, coef_out, res_out, coef_vmem, res_vmem, sem):
+    refs = [(coef, coef_vmem, coef_out)]
+    for i in range(MOVES):
+        part = pl.ds(i * (UNITS * UNIT // MOVES), UNITS * UNIT // MOVES)
+        refs.append((res.at[part], res_vmem.at[part], res_out.at[part]))
+    loads = [pltpu.make_async_copy(src, mid, sem.at[0, i]) for i, (src, mid, _) in enumerate(refs)]
+    stores = [pltpu.make_async_copy(mid, dst, sem.at[1, i]) for i, (_, mid, dst) in enumerate(refs)]
+    for copy in loads:
+        copy.start()
+    for load, store in zip(loads, stores):
+        load.wait()
+        store.start()
+    for copy in stores:
         copy.wait()
 
 
@@ -323,12 +339,13 @@
     chunks = len(CHUNKS)
     vmem = pl.BlockSpec(memory_space=pltpu.VMEM)
     hbm = pl.BlockSpec(memory_space=pl.ANY)
-    return pl.pallas_call(
+    outs = (
+        jax.ShapeDtypeStruct((TERMS, BLK, BLK), f32),
+        jax.ShapeDtypeStruct((entries, BLK, BLK), bf16),
+    )
+    coef, res = pl.pallas_call(
         kernel,
-        out_shape=(
-            jax.ShapeDtypeStruct((TERMS, BLK, BLK), f32),
-            jax.ShapeDtypeStruct((entries, BLK, BLK), bf16),
-        ),
+        out_shape=outs,
         in_specs=[hbm] * 3 + [vmem] * 4,
         out_specs=(hbm, hbm),
         scratch_shapes=[
@@ -342,7 +359,6 @@
             pltpu.VMEM((UNITS, N, UNIT, BLK), bf16),
             pltpu.VMEM((UNITS, N, UNIT, BLK), bf16),
             pltpu.VMEM((UNITS, TERMS * N, N * UNIT), bf16),
-            pltpu.VMEM((UNITS * 8, PAIR, TERMS * N), bf16),
             pltpu.VMEM((N * UNIT, BLK), f32),
             pltpu.VMEM((UNITS * 8, PAIR), f32),
             pltpu.VMEM((UNITS * 8, PAIR), f32),
@@ -350,7 +366,8 @@
             pltpu.VMEM((32, N), f32),
             pltpu.VMEM((len(PAIRS), N, BLK), f32),
             pltpu.VMEM((TERMS * N, BLK), f32),
-            pltpu.VMEM((TERMS * N, BLK), bf16),
+            pltpu.VMEM((BLK, TERMS * N), bf16),
+            pltpu.VMEM((TERMS, N, BLK), bf16),
             pltpu.VMEM((N, 8, BLK), bf16),
             pltpu.VMEM((N, 8, BLK), bf16),
             pltpu.VMEM((N * 8, BLK), f32),
@@ -376,6 +393,19 @@
         blocks, row_maps, col_maps, targets.reshape(1, entries), date_index.reshape(1, entries),
         jnp.asarray(table), jnp.asarray(products),
     )
+    return pl.pallas_call(
+        move,
+        out_shape=outs,
+        in_specs=[hbm] * 2,
+        out_specs=(hbm, hbm),
+        scratch_shapes=[
+            pltpu.VMEM((TERMS, BLK, BLK), f32),
+            pltpu.VMEM((entries, BLK, BLK), bf16),
+            dma((2, MOVES + 1)),
+        ],
+        compiler_params=pltpu.CompilerParams(vmem_limit_bytes=60 * 2**20),
+        name="move",
+    )(coef, res)
 
 
 def solution(mesh):

time: 95.9 us -> 79.2 us (0.83)
  Pallas kernels: 90 us -> 78.4 us
  local copies, waits for them, and re-layouts: 4.97 us -> 0 us
    pallas_call x1 -> x2, Pallas kernels: 90 us -> 78.4 us  [the longest x1 75.8 us: on_device(): pl.pallas_call(kernel, out_shape=outs, in_specs=[hbm] * 3 + [vmem] * 4, o...]
    unnamed x2 -> x0, local copies, waits for them, and re-layouts: 4.97 us -> none
where the time goes in v2:
time: 79.2 us; the launch traced here: 79 us
  Pallas kernels  78.4 us (99%)
    pallas_call x1, Pallas kernels, on_device(): pl.pallas_call(kernel, out_shape=outs, in_specs=[hbm] * 3 + [vmem] * 4, o...  75.8 us
    pallas_call x1, Pallas kernels, on_device(): pl.pallas_call(move, out_shape=outs, in_specs=[hbm] * 2, out_specs=(hbm,...  2.63 us

profile of v2, /device:TPU:1, one launch (start us, length us, event | category | flops | bytes accessed | tf_op | source)
XLA Modules:
  0.0 79.0 jit_solution(15599354111439476268)
XLA Ops:
  0.6 75.8 %fit.1 = (f32[7,128,128]{2,1,0:T(8,128)}, bf16[64,128,128]{2,1,0:T(8,128)(2,1)}) custom-call(bf16[64,128,128]{2,1,0:T(8,128)(2,1)} %b_hbm.1, bf16[64,128,128]{2,1,0:T(8,128)(2,1)} %r_hbm.1, bf16[64,128,128]{2,1,0:T(8,128)(2,1)} %c_hbm.1, s32[1,64]{1,0:T(1,128)} %bitcast.2, s32[1,64]{1,0:T(1,128)} %bitcast.3, f32[8,32]{1,0:T(8,128)} %constant.4.clone.table_ref, ...), custom_call_target="tpu_custom_call" | custom-call | tf_op jit(solution)/shard_map/fit/pallas_call | solution.py:346
  76.4 2.6 %move.1 = (f32[7,128,128]{2,1,0:T(8,128)}, bf16[64,128,128]{2,1,0:T(8,128)(2,1)}) custom-call(f32[7,128,128]{2,1,0:T(8,128)} %get-tuple-element.4.coef, bf16[64,128,128]{2,1,0:T(8,128)(2,1)} %get-tuple-element.5.res), custom_call_target="tpu_custom_call" | custom-call | tf_op jit(solution)/shard_map/move/pallas_call | solution.py:396

commit v3 on v2

--- a/solution.py
+++ b/solution.py
@@ -17,6 +17,7 @@
 PAIR = 256
 LOW = 16
 MOVES = 8
+BATCH = 8
 CHUNKS = ((0, 1), (1, 2), (3, 1))
 MESH = pl.DeviceIdType.MESH
 f32 = jnp.float32
@@ -72,7 +73,7 @@
     b_hbm, r_hbm, c_hbm, t_ref, d_ref, table_ref, products_ref,
     coef_hbm, res_hbm,
     bv, rv, cv, meta_own, meta, send1, recv1, send2, recv2, w, tmp,
-    trow, drow, tally, inv_rows, inv_full, moments, coefs_t, coefs, coef_send, coef_recv, ctmp, coef_out,
+    trow, drow, tally, inv_rows, inv_full, moments, coefs_t, coefs, coef_send, coef_recv, ctmp,
     load_sem, stage_sem, meta_ss, meta_rs, ss1, rs1, ss2, rs2, coef_ss, coef_rs, own_sem, out_sem,
 ):
     me = lax.axis_index("dev")
@@ -83,9 +84,8 @@
             pltpu.make_async_copy(src.at[part], dst.at[part], load_sem.at[i, u])
             for i, (src, dst) in enumerate(((b_hbm, bv), (c_hbm, cv), (r_hbm, rv)))
         ])
-    for group in loads:
-        for copy in group:
-            copy.start()
+    for copy in loads[0]:
+        copy.start()
 
     barrier = pltpu.get_barrier_semaphore()
     base = (me // LOW) * LOW
@@ -100,15 +100,38 @@
         peer = lax.rem(me + i * LOW, N)
         pl.semaphore_signal(barrier, inc=1, device_id=(peer,), device_id_type=MESH)
 
+    def greet():
+        pl.semaphore_wait(barrier, LOW - 1 + N // LOW - 1)
+
+        @pl.loop(1, N // LOW)
+        def _(i):
+            peer = lax.rem(me + i * LOW, N)
+            pl.semaphore_signal(stage_sem, inc=1, device_id=(peer,), device_id_type=MESH)
+
     def resample(u):
         for copy in loads[u]:
             copy.wait()
         for e in range(UNIT):
-            p = u * UNIT + e
-            half = lax.dot_general(
-                bv[p], cv[p], (((1,), (1,)), ((), ())), preferred_element_type=f32
-            ).astype(bf16)
-            tmp[pl.ds(e, BLK, stride=UNIT), :] = jnp.dot(rv[p], half, preferred_element_type=f32)
+            if u == 0 and e == 0:
+                for group in loads[1:]:
+                    for copy in group:
+                        copy.start()
+            if u == 0 and e == UNIT // 2:
+                greet()
+            if e % BATCH:
+                continue
+            batch = range(e, e + BATCH)
+            halves = [
+                lax.dot_general(
+                    bv[u * UNIT + i], cv[u * UNIT + i], (((1,), (1,)), ((), ())),
+                    preferred_element_type=f32,
+                ).astype(bf16)
+                for i in batch
+            ]
+            for i, half in zip(batch, halves):
+                tmp[pl.ds(i, BLK, stride=UNIT), :] = jnp.dot(
+                    rv[u * UNIT + i], half, preferred_element_type=f32
+                )
 
         @pl.loop(0, 8)
         def _(i):
@@ -137,13 +160,6 @@
     meta_own[0:1, 0:64] = t_ref[...]
     meta_own[0:1, 64:128] = d_ref[...]
     resample(0)
-    pl.semaphore_wait(barrier, LOW - 1 + N // LOW - 1)
-
-    @pl.loop(1, N // LOW)
-    def _(i):
-        peer = lax.rem(me + i * LOW, N)
-        pl.semaphore_signal(stage_sem, inc=1, device_id=(peer,), device_id_type=MESH)
-
     pl.semaphore_wait(stage_sem, N // LOW - 1)
 
     owns1 = []
@@ -237,9 +253,31 @@
             coefs[k, pl.ds(rows, 16), :] = value.astype(bf16)
             ctmp[pl.ds(rows * 8 + k, 16, stride=8), :] = value
         ctmp[pl.ds(rows * 8 + 7, 16, stride=8), :] = jnp.zeros((16, BLK), f32)
-        coef_send[pl.ds(rows, 16)] = (
-            ctmp[pl.ds(rows * 8, 128), :].astype(bf16).reshape(16, 8, BLK)
-        )
+
+    for k in range(TERMS):
+        coefs_t[:, k * N : (k + 1) * N] = coefs[k].T
+
+    def predict(u):
+        @pl.loop(0, 4)
+        def _(i):
+            lanes = pl.ds(pl.multiple_of(i * 512, 512), 512)
+            value = jnp.dot(coefs_t[...], w[u, :, lanes], preferred_element_type=f32)
+            send2[u, pl.ds(i * 32, 32)] = value.astype(bf16).T.reshape(32, UNIT, BLK)
+
+    owns2 = []
+    for c, (first, count) in enumerate(CHUNKS):
+        for u in range(first, first + count):
+            predict(u)
+        owns2.append(exchange(send2, recv2, ss2.at[c], rs2.at[c], first, count, 3 + c))
+
+    @pl.loop(0, UNITS * UNIT, unroll=4)
+    def _(p):
+        rv[p] = rv[p].T
+
+    @pl.loop(0, 8)
+    def _(i):
+        rows = ctmp[pl.ds(pl.multiple_of(i * 128, 128), 128), :]
+        coef_send[pl.ds(i * 16, 16)] = rows.astype(bf16).reshape(16, 8, BLK)
 
     own_coef = pltpu.make_async_copy(coef_send.at[me], coef_recv.at[me], own_sem.at[7])
     own_coef.start()
@@ -252,35 +290,7 @@
             send_sem=coef_ss, recv_sem=coef_rs, device_id=(peer,), device_id_type=MESH,
         ).start()
 
-    for k in range(TERMS):
-        coefs_t[:, k * N : (k + 1) * N] = coefs[k].T
-
-    def predict(u):
-        @pl.loop(0, 4)
-        def _(i):
-            lanes = pl.ds(pl.multiple_of(i * 512, 512), 512)
-            value = jnp.dot(coefs_t[...], w[u, :, lanes], preferred_element_type=f32)
-            send2[u, pl.ds(i * 32, 32)] = value.astype(bf16).T.reshape(32, UNIT, BLK)
-
-    owns2 = []
-    for c, (first, count) in enumerate(CHUNKS):
-        for u in range(first, first + count):
-            predict(u)
-        owns2.append(exchange(send2, recv2, ss2.at[c], rs2.at[c], first, count, 3 + c))
-
-    @pl.loop(0, UNITS * UNIT, unroll=4)
-    def _(p):
-        rv[p] = rv[p].T
-
-    part = coef_recv.at[pl.ds(0, N - 1)]
-    pltpu.make_async_copy(part, part, coef_rs).wait()
-    own_coef.wait()
-    ctmp[...] = coef_recv[...].astype(f32).reshape(N * 8, BLK)
-    for k in range(TERMS):
-        coef_out[k] = ctmp[pl.ds(k, N, stride=8), :]
-    outs = [pltpu.make_async_copy(coef_out, coef_hbm, out_sem.at[UNITS])]
-    outs[0].start()
-
+    outs = []
     for c, (first, count) in enumerate(CHUNKS):
         settle(recv2, rs2.at[c], first, count)
         owns2[c].wait()
@@ -290,15 +300,31 @@
                 rows = recv2[u, pl.ds(i * 16, 16)].astype(f32).reshape(256, BLK)
                 tmp[pl.ds(pl.multiple_of(i * 256, 256), 256), :] = rows
 
-            for e in range(UNIT):
-                p = u * UNIT + e
-                predicted = tmp[pl.ds(e, BLK, stride=UNIT), :].astype(bf16)
-                back = jnp.dot(predicted, cv[p], preferred_element_type=f32).astype(bf16)
-                adjoint = jnp.dot(rv[p], back, preferred_element_type=f32)
-                bv[p] = (bv[p].astype(f32) - adjoint).astype(bf16)
+            for e in range(0, UNIT, BATCH):
+                batch = range(e, e + BATCH)
+                backs = [
+                    jnp.dot(
+                        tmp[pl.ds(i, BLK, stride=UNIT), :].astype(bf16), cv[u * UNIT + i],
+                        preferred_element_type=f32,
+                    ).astype(bf16)
+                    for i in batch
+                ]
+                adjoints = [
+                    jnp.dot(rv[u * UNIT + i], back, preferred_element_type=f32)
+                    for i, back in zip(batch, backs)
+                ]
+                for i, adjoint in zip(batch, adjoints):
+                    p = u * UNIT + i
+                    bv[p] = (bv[p].astype(f32) - adjoint).astype(bf16)
             part = pl.ds(u * UNIT, UNIT)
             outs.append(pltpu.make_async_copy(bv.at[part], res_hbm.at[part], out_sem.at[u]))
             outs[-1].start()
+
+    part = coef_recv.at[pl.ds(0, N - 1)]
+    pltpu.make_async_copy(part, part, coef_rs).wait()
+    own_coef.wait()
+    outs.append(pltpu.make_async_copy(coef_recv, coef_hbm, out_sem.at[UNITS]))
+    outs[-1].start()
 
     part = meta.at[pl.ds(0, N - 1)]
     pltpu.make_async_copy(part, part, meta_ss).wait()
@@ -311,18 +337,17 @@
         copy.wait()
 
 
-def move(coef, res, coef_out, res_out, coef_vmem, res_vmem, sem):
-    refs = [(coef, coef_vmem, coef_out)]
+def finish(coef, res, coef_out, res_out, rows, planes, sem):
+    stores = []
     for i in range(MOVES):
         part = pl.ds(i * (UNITS * UNIT // MOVES), UNITS * UNIT // MOVES)
-        refs.append((res.at[part], res_vmem.at[part], res_out.at[part]))
-    loads = [pltpu.make_async_copy(src, mid, sem.at[0, i]) for i, (src, mid, _) in enumerate(refs)]
-    stores = [pltpu.make_async_copy(mid, dst, sem.at[1, i]) for i, (_, mid, dst) in enumerate(refs)]
-    for copy in loads:
-        copy.start()
-    for load, store in zip(loads, stores):
-        load.wait()
-        store.start()
+        stores.append(pltpu.make_async_copy(res.at[part], res_out.at[part], sem.at[i]))
+        stores[-1].start()
+    rows[...] = coef[...].astype(f32).reshape(N * 8, BLK)
+    for k in range(TERMS):
+        planes[k] = rows[pl.ds(k, N, stride=8), :]
+    stores.append(pltpu.make_async_copy(planes, coef_out, sem.at[MOVES]))
+    stores[-1].start()
     for copy in stores:
         copy.wait()
 
@@ -345,7 +370,7 @@
     )
     coef, res = pl.pallas_call(
         kernel,
-        out_shape=outs,
+        out_shape=(pltpu.VMEM((N, 8, BLK), bf16), pltpu.VMEM((entries, BLK, BLK), bf16)),
         in_specs=[hbm] * 3 + [vmem] * 4,
         out_specs=(hbm, hbm),
         scratch_shapes=[
@@ -371,7 +396,6 @@
             pltpu.VMEM((N, 8, BLK), bf16),
             pltpu.VMEM((N, 8, BLK), bf16),
             pltpu.VMEM((N * 8, BLK), f32),
-            pltpu.VMEM((TERMS, N, BLK), f32),
             dma((3, UNITS)),
             pltpu.SemaphoreType.REGULAR,
             dma,
@@ -386,25 +410,25 @@
             dma((UNITS + 1,)),
         ],
         compiler_params=pltpu.CompilerParams(
-            collective_id=0, has_side_effects=True, vmem_limit_bytes=58 * 2**20
+            collective_id=0, has_side_effects=True, vmem_limit_bytes=52 * 2**20
         ),
         name="fit",
     )(
-        blocks, row_maps, col_maps, targets.reshape(1, entries), date_index.reshape(1, entries),
+        *[pltpu.with_memory_space_constraint(x, pltpu.HBM) for x in (blocks, row_maps, col_maps)], targets.reshape(1, entries), date_index.reshape(1, entries),
         jnp.asarray(table), jnp.asarray(products),
     )
     return pl.pallas_call(
-        move,
+        finish,
         out_shape=outs,
-        in_specs=[hbm] * 2,
+        in_specs=[vmem] * 2,
         out_specs=(hbm, hbm),
         scratch_shapes=[
+            pltpu.VMEM((N * 8, BLK), f32),
             pltpu.VMEM((TERMS, BLK, BLK), f32),
-            pltpu.VMEM((entries, BLK, BLK), bf16),
-            dma((2, MOVES + 1)),
+            dma((MOVES + 1,)),
         ],
-        compiler_params=pltpu.CompilerParams(vmem_limit_bytes=60 * 2**20),
-        name="move",
+        compiler_params=pltpu.CompilerParams(vmem_limit_bytes=16 * 2**20),
+        name="finish",
     )(coef, res)
 
 

time: 79.2 us -> 76.1 us (0.961)
  Pallas kernels: 78.4 us -> 75.3 us
    pallas_call x2, Pallas kernels: 78.4 us -> 75.3 us  [the longest x1 73.7 us: on_device(): pl.pallas_call(kernel, out_shape=(pltpu.VMEM((N, 8, BLK), bf16), pltpu.VM...]
where the time goes in v3:
time: 76.1 us; the launch traced here: 75.9 us
  Pallas kernels  75.3 us (99%)
    pallas_call x1, Pallas kernels, on_device(): pl.pallas_call(kernel, out_shape=(pltpu.VMEM((N, 8, BLK), bf16), pltpu.VM...  73.7 us
    pallas_call x1, Pallas kernels, on_device(): pl.pallas_call(finish, out_shape=outs, in_specs=[vmem] * 2, out_specs=(hb...  1.54 us

profile of v3, /device:TPU:1, one launch (start us, length us, event | category | flops | bytes accessed | tf_op | source)
XLA Modules:
  0.0 75.9 jit_solution(13052166564885819957)
XLA Ops:
  0.6 73.7 %fit.1 = (bf16[128,8,128]{2,1,0:T(8,128)(2,1)S(1)}, bf16[64,128,128]{2,1,0:T(8,128)(2,1)S(1)}) custom-call(bf16[64,128,128]{2,1,0:T(8,128)(2,1)} %b_hbm.1, bf16[64,128,128]{2,1,0:T(8,128)(2,1)} %r_hbm.1, bf16[64,128,128]{2,1,0:T(8,128)(2,1)} %c_hbm.1, s32[1,64]{1,0:T(1,128)} %bitcast.2, s32[1,64]{1,0:T(1,128)} %bitcast.3, f32[8,32]{1,0:T(8,128)} %constant.4.clone.table_ref, ...), custom_call_target="tpu_custom_call" | custom-call | tf_op jit(solution)/shard_map/fit/pallas_call | solution.py:371
  74.4 1.5 %finish.1 = (f32[7,128,128]{2,1,0:T(8,128)}, bf16[64,128,128]{2,1,0:T(8,128)(2,1)}) custom-call(bf16[128,8,128]{2,1,0:T(8,128)(2,1)S(1)} %get-tuple-element.4.coef, bf16[64,128,128]{2,1,0:T(8,128)(2,1)S(1)} %get-tuple-element.5.res), custom_call_target="tpu_custom_call" | custom-call | tf_op jit(solution)/shard_map/finish/pallas_call | solution.py:420

commit v4 on v3

--- a/solution.py
+++ b/solution.py
@@ -15,7 +15,6 @@
 UNIT = 16
 UNITS = 4
 PAIR = 256
-LOW = 16
 MOVES = 8
 BATCH = 8
 CHUNKS = ((0, 1), (1, 2), (3, 1))
@@ -71,10 +70,10 @@
 
 def kernel(
     b_hbm, r_hbm, c_hbm, t_ref, d_ref, table_ref, products_ref,
-    coef_hbm, res_hbm,
+    coef_ref, res_ref,
     bv, rv, cv, meta_own, meta, send1, recv1, send2, recv2, w, tmp,
     trow, drow, tally, inv_rows, inv_full, moments, coefs_t, coefs, coef_send, coef_recv, ctmp,
-    load_sem, stage_sem, meta_ss, meta_rs, ss1, rs1, ss2, rs2, coef_ss, coef_rs, own_sem, out_sem,
+    load_sem, meta_ss, meta_rs, ss1, rs1, ss2, rs2, coef_ss, coef_rs, own_sem,
 ):
     me = lax.axis_index("dev")
     loads = []
@@ -88,25 +87,11 @@
         copy.start()
 
     barrier = pltpu.get_barrier_semaphore()
-    base = (me // LOW) * LOW
-
-    @pl.loop(1, LOW)
+
+    @pl.loop(1, N, unroll=4)
     def _(i):
-        peer = base + lax.rem(me + i, LOW)
+        peer = lax.rem(me + i * 45, N)
         pl.semaphore_signal(barrier, inc=1, device_id=(peer,), device_id_type=MESH)
-
-    @pl.loop(1, N // LOW)
-    def _(i):
-        peer = lax.rem(me + i * LOW, N)
-        pl.semaphore_signal(barrier, inc=1, device_id=(peer,), device_id_type=MESH)
-
-    def greet():
-        pl.semaphore_wait(barrier, LOW - 1 + N // LOW - 1)
-
-        @pl.loop(1, N // LOW)
-        def _(i):
-            peer = lax.rem(me + i * LOW, N)
-            pl.semaphore_signal(stage_sem, inc=1, device_id=(peer,), device_id_type=MESH)
 
     def resample(u):
         for copy in loads[u]:
@@ -116,8 +101,6 @@
                 for group in loads[1:]:
                     for copy in group:
                         copy.start()
-            if u == 0 and e == UNIT // 2:
-                greet()
             if e % BATCH:
                 continue
             batch = range(e, e + BATCH)
@@ -133,7 +116,7 @@
                     rv[u * UNIT + i], half, preferred_element_type=f32
                 )
 
-        @pl.loop(0, 8)
+        @pl.loop(0, 8, unroll=8)
         def _(i):
             rows = tmp[pl.ds(pl.multiple_of(i * 256, 256), 256), :]
             send1[u, pl.ds(i * 16, 16)] = rows.astype(bf16).reshape(16, UNIT, BLK)
@@ -145,7 +128,7 @@
 
         @pl.loop(1, N, unroll=4)
         def _(i):
-            peer = lax.rem(me + i * 37, N)
+            peer = lax.rem(me + i * 45, N)
             pltpu.make_async_remote_copy(
                 src_ref=src.at[units, peer], dst_ref=dst.at[units, me],
                 send_sem=ss, recv_sem=rs, device_id=(peer,), device_id_type=MESH,
@@ -160,7 +143,7 @@
     meta_own[0:1, 0:64] = t_ref[...]
     meta_own[0:1, 64:128] = d_ref[...]
     resample(0)
-    pl.semaphore_wait(stage_sem, N // LOW - 1)
+    pl.semaphore_wait(barrier, N - 1)
 
     owns1 = []
     for c, (first, count) in enumerate(CHUNKS):
@@ -174,7 +157,7 @@
 
             @pl.loop(1, N, unroll=4)
             def _(i):
-                peer = lax.rem(me + i * 37, N)
+                peer = lax.rem(me + i * 45, N)
                 pltpu.make_async_remote_copy(
                     src_ref=meta_own, dst_ref=meta.at[me],
                     send_sem=meta_ss, recv_sem=meta_rs, device_id=(peer,), device_id_type=MESH,
@@ -199,7 +182,7 @@
 
     @pl.loop(0, UNITS)
     def _(u):
-        @pl.loop(0, 8)
+        @pl.loop(0, 8, unroll=2)
         def _(g):
             pair = u * 8 + g
             tile = trow[pl.ds(pair, 1), :]
@@ -242,7 +225,7 @@
     for i, (k, l) in enumerate(PAIRS):
         at[k, l] = at[l, k] = i
 
-    @pl.loop(0, N // 16)
+    @pl.loop(0, N // 16, unroll=2)
     def _(i):
         rows = pl.multiple_of(i * 16, 16)
         given = [moments[pl.ds(l * N + rows, 16), :] for l in range(TERMS)]
@@ -258,7 +241,7 @@
         coefs_t[:, k * N : (k + 1) * N] = coefs[k].T
 
     def predict(u):
-        @pl.loop(0, 4)
+        @pl.loop(0, 4, unroll=4)
         def _(i):
             lanes = pl.ds(pl.multiple_of(i * 512, 512), 512)
             value = jnp.dot(coefs_t[...], w[u, :, lanes], preferred_element_type=f32)
@@ -284,18 +267,17 @@
 
     @pl.loop(1, N, unroll=4)
     def _(i):
-        peer = lax.rem(me + i * 37, N)
+        peer = lax.rem(me + i * 45, N)
         pltpu.make_async_remote_copy(
             src_ref=coef_send.at[peer], dst_ref=coef_recv.at[me],
             send_sem=coef_ss, recv_sem=coef_rs, device_id=(peer,), device_id_type=MESH,
         ).start()
 
-    outs = []
     for c, (first, count) in enumerate(CHUNKS):
         settle(recv2, rs2.at[c], first, count)
         owns2[c].wait()
         for u in range(first, first + count):
-            @pl.loop(0, 8)
+            @pl.loop(0, 8, unroll=8)
             def _(i):
                 rows = recv2[u, pl.ds(i * 16, 16)].astype(f32).reshape(256, BLK)
                 tmp[pl.ds(pl.multiple_of(i * 256, 256), 256), :] = rows
@@ -315,16 +297,12 @@
                 ]
                 for i, adjoint in zip(batch, adjoints):
                     p = u * UNIT + i
-                    bv[p] = (bv[p].astype(f32) - adjoint).astype(bf16)
-            part = pl.ds(u * UNIT, UNIT)
-            outs.append(pltpu.make_async_copy(bv.at[part], res_hbm.at[part], out_sem.at[u]))
-            outs[-1].start()
+                    res_ref[p] = (bv[p].astype(f32) - adjoint).astype(bf16)
 
     part = coef_recv.at[pl.ds(0, N - 1)]
     pltpu.make_async_copy(part, part, coef_rs).wait()
     own_coef.wait()
-    outs.append(pltpu.make_async_copy(coef_recv, coef_hbm, out_sem.at[UNITS]))
-    outs[-1].start()
+    coef_ref[...] = coef_recv[...]
 
     part = meta.at[pl.ds(0, N - 1)]
     pltpu.make_async_copy(part, part, meta_ss).wait()
@@ -333,8 +311,6 @@
     for c, (first, count) in enumerate(CHUNKS):
         settle(send1, ss1.at[c], first, count)
         settle(send2, ss2.at[c], first, count)
-    for copy in outs:
-        copy.wait()
 
 
 def finish(coef, res, coef_out, res_out, rows, planes, sem):
@@ -372,7 +348,7 @@
         kernel,
         out_shape=(pltpu.VMEM((N, 8, BLK), bf16), pltpu.VMEM((entries, BLK, BLK), bf16)),
         in_specs=[hbm] * 3 + [vmem] * 4,
-        out_specs=(hbm, hbm),
+        out_specs=(vmem, vmem),
         scratch_shapes=[
             pltpu.VMEM((entries, BLK, BLK), bf16),
             pltpu.VMEM((entries, BLK, BLK), bf16),
@@ -397,7 +373,6 @@
             pltpu.VMEM((N, 8, BLK), bf16),
             pltpu.VMEM((N * 8, BLK), f32),
             dma((3, UNITS)),
-            pltpu.SemaphoreType.REGULAR,
             dma,
             dma,
             dma((chunks,)),
@@ -407,7 +382,6 @@
             dma,
             dma,
             dma((8,)),
-            dma((UNITS + 1,)),
         ],
         compiler_params=pltpu.CompilerParams(
             collective_id=0, has_side_effects=True, vmem_limit_bytes=52 * 2**20

time: 76.1 us -> 75.7 us (level)
  no operation moved by 1% of the time
where the time goes in v4:
time: 75.7 us; the launch traced here: 75.5 us
  Pallas kernels  74.8 us (99%)
  between operations  0.8 us (1%)
    pallas_call x1, Pallas kernels, on_device(): pl.pallas_call(kernel, out_shape=(pltpu.VMEM((N, 8, BLK), bf16), pltpu.VM...  73.2 us
    pallas_call x1, Pallas kernels, on_device(): pl.pallas_call(finish, out_shape=outs, in_specs=[vmem] * 2, out_specs=(hb...  1.54 us

profile of v4, /device:TPU:1, one launch (start us, length us, event | category | flops | bytes accessed | tf_op | source)
XLA Modules:
  0.0 75.5 jit_solution(18090717170329778013)
XLA Ops:
  0.6 73.2 %fit.1 = (bf16[128,8,128]{2,1,0:T(8,128)(2,1)S(1)}, bf16[64,128,128]{2,1,0:T(8,128)(2,1)S(1)}) custom-call(bf16[64,128,128]{2,1,0:T(8,128)(2,1)} %b_hbm.1, bf16[64,128,128]{2,1,0:T(8,128)(2,1)} %r_hbm.1, bf16[64,128,128]{2,1,0:T(8,128)(2,1)} %c_hbm.1, s32[1,64]{1,0:T(1,128)} %bitcast.2, s32[1,64]{1,0:T(1,128)} %bitcast.3, f32[8,32]{1,0:T(8,128)} %constant.4.clone.table_ref, ...), custom_call_target="tpu_custom_call" | custom-call | tf_op jit(solution)/shard_map/fit/pallas_call | solution.py:347
  73.9 1.5 %finish.1 = (f32[7,128,128]{2,1,0:T(8,128)}, bf16[64,128,128]{2,1,0:T(8,128)(2,1)}) custom-call(bf16[128,8,128]{2,1,0:T(8,128)(2,1)S(1)} %get-tuple-element.4.coef, bf16[64,128,128]{2,1,0:T(8,128)(2,1)S(1)} %get-tuple-element.5.res), custom_call_target="tpu_custom_call" | custom-call | tf_op jit(solution)/shard_map/finish/pallas_call | solution.py:394

commit v5 on v4

--- a/solution.py
+++ b/solution.py
@@ -16,7 +16,7 @@
 UNITS = 4
 PAIR = 256
 MOVES = 8
-BATCH = 8
+BATCH = 16
 CHUNKS = ((0, 1), (1, 2), (3, 1))
 MESH = pl.DeviceIdType.MESH
 f32 = jnp.float32

time: 75.7 us -> 75.7 us (level)
  no operation moved by 1% of the time
where the time goes in v5:
time: 75.7 us; the launch traced here: 75.5 us
  Pallas kernels  74.8 us (99%)
  between operations  0.8 us (1%)
    pallas_call x1, Pallas kernels, on_device(): pl.pallas_call(kernel, out_shape=(pltpu.VMEM((N, 8, BLK), bf16), pltpu.VM...  73.2 us
    pallas_call x1, Pallas kernels, on_device(): pl.pallas_call(finish, out_shape=outs, in_specs=[vmem] * 2, out_specs=(hb...  1.54 us

profile of v5, /device:TPU:1, one launch (start us, length us, event | category | flops | bytes accessed | tf_op | source)
XLA Modules:
  0.0 75.5 jit_solution(10049377356852173066)
XLA Ops:
  0.6 73.2 %fit.1 = (bf16[128,8,128]{2,1,0:T(8,128)(2,1)S(1)}, bf16[64,128,128]{2,1,0:T(8,128)(2,1)S(1)}) custom-call(bf16[64,128,128]{2,1,0:T(8,128)(2,1)} %b_hbm.1, bf16[64,128,128]{2,1,0:T(8,128)(2,1)} %r_hbm.1, bf16[64,128,128]{2,1,0:T(8,128)(2,1)} %c_hbm.1, s32[1,64]{1,0:T(1,128)} %bitcast.2, s32[1,64]{1,0:T(1,128)} %bitcast.3, f32[8,32]{1,0:T(8,128)} %constant.4.clone.table_ref, ...), custom_call_target="tpu_custom_call" | custom-call | tf_op jit(solution)/shard_map/fit/pallas_call | solution.py:347
  73.9 1.5 %finish.1 = (f32[7,128,128]{2,1,0:T(8,128)}, bf16[64,128,128]{2,1,0:T(8,128)(2,1)}) custom-call(bf16[128,8,128]{2,1,0:T(8,128)(2,1)S(1)} %get-tuple-element.4.coef, bf16[64,128,128]{2,1,0:T(8,128)(2,1)S(1)} %get-tuple-element.5.res), custom_call_target="tpu_custom_call" | custom-call | tf_op jit(solution)/shard_map/finish/pallas_call | solution.py:394
